TPU v7x, 32 devices: a whole 2x2x4 slice. The times are simulated.
32 devices in a mesh: job: 2 (over x), tok: 16 (over z, y, core).
Axes of the slice: x: 2, y: 2, z: 4, core: 2. Of those that a mesh axis runs over, the one named last changes fastest.
Arguments:
- pair_states: bfloat16 [1024, 512, 128], P(('job', 'tok')), parts along dimension 0, may hold values from -6 to 6
- weight_in: bfloat16 [128, 1024], replicated, may hold values from -0.5 to 0.5
- weight_out: bfloat16 [512, 128], replicated, may hold values from -0.25 to 0.25
- weight_bias: bfloat16 [2, 128, 16], replicated, may hold values from -0.5 to 0.5
- key_mask: int32 [1024], P('job'), parts along dimension 0, may hold values 0 or 1
- noise_level: int32 [4], P('job'), parts along dimension 0, may hold values from 0 to 199
- query_states: bfloat16 [2, 16, 4, 48, 512], P(None, 'tok', 'job'), parts along dimension 2, may hold values from -16 to 16
- key_states: bfloat16 [2, 16, 4, 48, 512], P(None, 'tok', 'job'), parts along dimension 2, may hold values from -16 to 16
- value_states: bfloat16 [2, 16, 4, 48, 512], P(None, 'tok', 'job'), parts along dimension 2, may hold values from -6 to 6
- output_grad: bfloat16 [2, 16, 4, 48, 512], P(None, 'tok', 'job'), parts along dimension 2, may hold values from -6 to 6
Outputs:
- pair_grad: bfloat16 [1024, 512, 128], P(('job', 'tok')), parts along dimension 0
- query_grad: bfloat16 [2, 16, 4, 48, 512], P(None, 'tok', 'job'), parts along dimension 2
- key_grad: bfloat16 [2, 16, 4, 48, 512], P(None, 'tok', 'job'), parts along dimension 2
- value_grad: bfloat16 [2, 16, 4, 48, 512], P(None, 'tok', 'job'), parts along dimension 2
- weight_in_grad: float32 [256, 1024], P('job'), parts along dimension 0
- weight_out_grad: float32 [1024, 128], P('job'), parts along dimension 0
- weight_bias_grad: float32 [4, 128, 16], P('job'), parts along dimension 0
There are 2 independent parts, one for each index of `job`. A program takes and returns all parts, laid end to end along the dimension named above; an argument that names none is the same for every part. Nothing has to cross between parts.
All inputs are finite; a program needn't handle non-finite values.
Results may differ from a plain program's by a relative error of at most 0.015.
Values may be sent and summed in bfloat16 or wider, within the bound.
No kernel may reach another device: no remote copies, remote signals or barrier semaphores. Data moves between devices by JAX's collectives and lax.ppermute only.
A program may use at most 192 MiB of HBM per device.

v0:
```python
import functools
import math

import jax
import jax.numpy as jnp
from jax import lax
from jax.experimental import pallas as pl
from jax.experimental.pallas import tpu as pltpu
from jax.sharding import PartitionSpec as P

LEVELS = 200


sigma_high = 160.0
sigma_low = 0.0004
sigma_data = 16.0
rho_power = 7.0
epsilon = 1e-05
masked_score = -1000000000.0

F32 = jnp.float32
BF16 = jnp.bfloat16


def sample_weight(levels):
    level = levels.astype(jnp.float32)
    top_root = sigma_high ** (1.0 / rho_power)
    low_root = sigma_low ** (1.0 / rho_power)
    sigma_level = (top_root + level / (LEVELS - 1) * (low_root - top_root)) ** rho_power
    return (sigma_level * sigma_level + sigma_data * sigma_data) / (sigma_level + sigma_data) ** 2


def mm(left, right, left_dim=1, right_dim=0):
    return lax.dot_general(
        left, right, (((left_dim,), (right_dim,)), ((), ())), preferred_element_type=F32
    )


def normalize(inputs):
    centered = inputs - jnp.mean(inputs, 0, keepdims=True)
    inv_std = lax.rsqrt(jnp.mean(centered * centered, 0, keepdims=True) + epsilon)
    return centered * inv_std, inv_std


def norm_back(normed, inv_std, upstream):
    return inv_std * (
        upstream
        - jnp.mean(upstream, 0, keepdims=True)
        - normed * jnp.mean(upstream * normed, 0, keepdims=True)
    )


def split_width(width):
    return 256 if width % 256 == 0 else width


def interleave(make_stages, count, lag):
    rows = [make_stages(index) for index in range(count)]
    running = []
    clock = 0
    while rows or running:
        while rows and clock >= lag * (count - len(rows)):
            running.append(rows.pop(0))
        running = [row for row in running if next(row, None) is not None]
        clock += 1


def for_groups(count, group, one_group):
    group = math.gcd(count, group)

    def step(at, carry):
        one_group(at * group, group)
        return carry

    if count == group:
        step(0, 0)
    else:
        lax.fori_loop(0, count // group, step, 0)


def row_step(rows):
    return math.gcd(rows, 8 if rows > 8 else 4)


def is_direct(rows, crop):
    return rows % 8 == 0 and crop % 128 == 0


def forward_kernel(direct, first, pair_ref, w_bias_ref, *refs):
    refs = list(refs)
    if first:
        w_in_ref, w_out_ref = refs.pop(0), refs.pop(0)
    else:
        w_in_t_ref, w_out_t_ref = refs.pop(0), refs.pop(0)
    bias_ref = refs.pop(0)
    if first:
        w_in_t_ref, w_out_t_ref = refs.pop(0), refs.pop(0)
    lines_ref = refs.pop(0)
    width = w_out_t_ref.shape[1]
    layers, heads, channels = w_bias_ref.shape
    piece = split_width(width)
    step = pair_ref.shape[0]
    first_row = pl.program_id(0) * step

    if first:

        @pl.when(pl.program_id(0) == 0)
        def _():
            w_in_t = w_in_ref[...].T
            w_in_t_ref[:width, :] = w_in_t[:width] * 0.5
            w_in_t_ref[width:, :] = w_in_t[width:]
            w_out_t_ref[...] = w_out_ref[...].T

    def stages(row):
        pair_float = pair_ref[row].T.astype(F32)
        normed_in = normalize(pair_float)[0].astype(BF16)
        yield True
        hiddens = []
        for at in range(0, width, piece):
            half_gate = mm(w_in_t_ref[at : at + piece, :], normed_in)
            up_in = mm(w_in_t_ref[width + at : width + at + piece, :], normed_in)
            yield True
            hidden = half_gate * (1.0 + jnp.tanh(half_gate)) * up_in
            hiddens.append(hidden.astype(BF16))
            yield True
        lifted = pair_float + mm(w_out_t_ref[...], jnp.concatenate(hiddens, 0))
        yield True
        normed_out = normalize(lifted)[0].astype(BF16)
        yield True
        bias = mm(w_bias_ref[...].reshape(layers * heads, channels), normed_out)
        if direct:
            tiles, total, tile = lines_ref.shape
            rows = total // (layers * heads)
            for layer in range(layers):
                at = pl.ds(layer * rows + first_row + row, heads, stride=layers * rows)
                lines = bias[layer * heads : (layer + 1) * heads]
                for index in range(tiles):
                    lines_ref[index, at, :] = lines[:, index * tile : (index + 1) * tile]
        else:
            bias_ref[row] = bias.astype(BF16)

    for_groups(step, 8, lambda at, count: interleave(lambda i: stages(at + i), count, 0))

    if direct:

        @pl.when(pl.program_id(0) == pl.num_programs(0) - 1)
        def _():
            tiles, _, tile = lines_ref.shape
            for index in range(tiles):
                lines = lines_ref[index].reshape(bias_ref.shape[:2] + (tile,))
                bias_ref[:, :, index * tile : (index + 1) * tile] = lines.astype(BF16)


def whole_spec(array):
    return pl.BlockSpec(array.shape, lambda i: (0,) * len(array.shape))


def forward_rows(start, rows, pair, w_in, w_out, w_bias, prepared):
    crop, channels = pair.shape[1:]
    layers, heads, _ = w_bias.shape
    lanes = layers * heads
    step = row_step(rows)
    first_step = start // step
    positions = rows * crop
    width = w_out.shape[0]
    direct = is_direct(rows, crop)
    first = prepared is None
    line_shape = (lanes, rows, crop) if direct else (rows, lanes, crop)
    shapes = [jax.ShapeDtypeStruct(line_shape, BF16)]
    out_specs = [
        whole_spec(shapes[0])
        if direct
        else pl.BlockSpec((step, lanes, crop), lambda i: (i, 0, 0))
    ]
    operands = [pair, w_bias, *((w_in, w_out) if first else prepared)]
    if first:
        for shape in (w_in.shape[::-1], w_out.shape[::-1]):
            shapes.append(jax.ShapeDtypeStruct(shape, BF16))
            out_specs.append(whole_spec(shapes[-1]))
    return pl.pallas_call(
        functools.partial(forward_kernel, direct, first),
        grid=(rows // step,),
        in_specs=[pl.BlockSpec((step, crop, channels), lambda i: (first_step + i, 0, 0))]
        + [whole_spec(array) for array in operands[1:]],
        out_specs=out_specs,
        out_shape=shapes,
        scratch_shapes=[
            pltpu.VMEM((crop // 128, lanes * rows, 128) if direct else (1, 8, 128), F32),
        ],
        compiler_params=pltpu.CompilerParams(vmem_limit_bytes=56 * 2**20),
        cost_estimate=pl.CostEstimate(
            flops=6 * positions * channels * (3 * width + lanes),
            bytes_accessed=positions * (channels + lanes) * 2,
            transcendentals=positions * width,
        ),
        name="pair_forward",
    )(*operands)


def backward_kernel(
    first,
    last,
    direct,
    pair_ref,
    d_bias_ref,
    w_bias_ref,
    w_in_t_ref,
    w_out_t_ref,
    w_back_ref,
    w_half_ref,
    *refs,
):
    outs = list(refs[:-1])
    parity_ref = outs.pop(0) if last else None
    if not first:
        before_ref = outs.pop(0)
        outs.pop(0)
    pair_grad_ref, sums_ref = outs.pop(0), outs.pop(0)
    lines_ref = refs[-1]
    width = w_half_ref.shape[0]
    layers, heads, channels = w_bias_ref.shape
    lanes = layers * heads
    piece = split_width(width)
    step = pair_ref.shape[0]
    one, two = jnp.asarray(1.0, BF16), jnp.asarray(2.0, BF16)
    first_row = pl.program_id(0) * step

    @pl.when(pl.program_id(0) == 0)
    def _():
        if first:
            sums_ref[...] = jnp.zeros_like(sums_ref)
        else:
            sums_ref[...] = before_ref[...]
        if direct:
            tiles, total, tile = lines_ref.shape
            for index in range(tiles):
                lines = d_bias_ref[:, :, index * tile : (index + 1) * tile].astype(F32)
                lines_ref[index] = lines.reshape(total, tile)

    def read_lines(row):
        if not direct:
            return d_bias_ref[row]
        tiles, total, _ = lines_ref.shape
        rows = total // lanes
        found = []
        for layer in range(layers):
            at = pl.ds(layer * rows + first_row + row, heads, stride=layers * rows)
            found.append(jnp.concatenate([lines_ref[index, at, :] for index in range(tiles)], 1))
        return jnp.concatenate(found, 0).astype(BF16)

    def add_sums(at, left, right):
        sums_ref[at : at + left.shape[0], :] += mm(left, right, 1, 1)

    def stages(row):
        pair_float = pair_ref[row].T.astype(F32)
        normed_float, inv_in = normalize(pair_float)
        normed_in = normed_float.astype(BF16)
        yield True
        kept = []
        for at in range(0, width, piece):
            half_gate = mm(w_in_t_ref[at : at + piece, :], normed_in)
            up_in = mm(w_in_t_ref[width + at : width + at + piece, :], normed_in)
            yield True
            one_plus = (1.0 + jnp.tanh(half_gate)).astype(BF16)
            half_gate, up_in = half_gate.astype(BF16), up_in.astype(BF16)
            silu = half_gate * one_plus
            hidden = silu * up_in
            slope = one_plus * (one + half_gate * (two - one_plus)) * up_in
            kept.append((silu, slope, hidden))
            yield True
        hidden = jnp.concatenate([hidden for _, _, hidden in kept], 0)
        lifted = pair_float + mm(w_out_t_ref[...], hidden)
        yield True
        out_float, inv_out = normalize(lifted)
        normed_out = out_float.astype(BF16)
        yield True
        d_bias = read_lines(row)
        d_normed = mm(w_bias_ref[...].reshape(lanes, channels), d_bias, 0, 0)
        add_sums(3 * width, d_bias, normed_out)
        d_lifted = norm_back(out_float, inv_out, d_normed)
        lifted_half = d_lifted.astype(BF16)
        yield True
        d_normed_in = None
        for index, (silu, slope, hidden) in enumerate(kept):
            at = index * piece
            d_hidden = mm(w_half_ref[at : at + piece, :], lifted_half).astype(BF16)
            add_sums(2 * width + at, hidden, lifted_half)
            yield True
            d_both = jnp.concatenate([d_hidden * slope, d_hidden * silu], 0)
            add_sums(2 * at, d_both, normed_in)
            part = mm(w_back_ref[:, 2 * at : 2 * at + 2 * piece], d_both)
            d_normed_in = part if d_normed_in is None else d_normed_in + part
            yield True
        pair_grad = d_lifted + norm_back(normed_float, inv_in, d_normed_in)
        pair_grad_ref[row] = pair_grad.astype(BF16).T

    for_groups(step, 8, lambda at, count: interleave(lambda i: stages(at + i), count, 0))

    if last:
        keep_ref, send_ref = outs

        @pl.when(pl.program_id(0) == pl.num_programs(0) - 1)
        def _():
            half = sums_ref.shape[0] // 2
            parity = parity_ref[0]
            gates, ups = [], []
            for at in range(0, 2 * width, 2 * piece):
                gates.append(sums_ref[at : at + piece, :])
                ups.append(2.0 * sums_ref[at + piece : at + 2 * piece, :])
            sums_ref[: 2 * width, :] = jnp.concatenate(gates + ups, 0)
            keep_ref[...] = sums_ref[pl.ds(pl.multiple_of(parity * half, 8), half), :]
            other = pl.ds(pl.multiple_of((1 - parity) * half, 8), half)
            send_ref[...] = sums_ref[other, :].astype(BF16)


def backward_rows(start, rows, direct, sum_rows, pair, d_bias, w_bias, prepared, state, parity):
    crop, channels = pair.shape[1:]
    layers, heads, _ = w_bias.shape
    lanes = layers * heads
    width = prepared[3].shape[0]
    step = row_step(rows)
    first_step = start // step
    positions = rows * crop
    first, last = start == 0, start + rows == pair.shape[0]
    pair_spec = pl.BlockSpec((step, crop, channels), lambda i: (first_step + i, 0, 0))
    line_spec = whole_spec(d_bias) if direct else pl.BlockSpec((step, lanes, crop), lambda i: (i, 0, 0))
    operands = [pair, d_bias, w_bias, *prepared]
    in_specs = [pair_spec, line_spec] + [whole_spec(array) for array in operands[2:]]
    aliases = {}
    if last:
        operands.append(parity)
        in_specs.append(pl.BlockSpec(memory_space=pltpu.SMEM))
    if not first:
        pair_grad, sums = state
        operands += [sums, pair_grad]
        in_specs += [whole_spec(sums), pl.BlockSpec(memory_space=pl.ANY)]
        aliases = {len(operands) - 1: 0}
    shapes = [
        jax.ShapeDtypeStruct(pair.shape, BF16),
        jax.ShapeDtypeStruct((sum_rows, channels), F32),
    ]
    if last:
        shapes.append(jax.ShapeDtypeStruct((sum_rows // 2, channels), F32))
        shapes.append(jax.ShapeDtypeStruct((sum_rows // 2, channels), BF16))
    out_specs = [pair_spec] + [whole_spec(shape) for shape in shapes[1:]]
    line_rows = lanes * d_bias.shape[1]
    return pl.pallas_call(
        functools.partial(backward_kernel, first, last, direct),
        grid=(rows // step,),
        in_specs=in_specs,
        out_specs=out_specs,
        out_shape=shapes,
        input_output_aliases=aliases,
        scratch_shapes=[
            pltpu.VMEM((crop // 128, line_rows, 128) if direct else (1, 8, 128), F32),
        ],
        compiler_params=pltpu.CompilerParams(vmem_limit_bytes=56 * 2**20),
        cost_estimate=pl.CostEstimate(
            flops=6 * positions * channels * (9 * width + 2 * lanes),
            bytes_accessed=positions * (2 * channels + lanes) * 2,
            transcendentals=positions * width,
        ),
        name="pair_backward",
    )(*operands)


def attend_kernel(
    first, last, weight_ref, bias_ref, valid_ref, q_ref, k_ref, v_ref, g_ref, *refs
):
    if first:
        dq_ref, dk_ref, dv_ref, d_bias_ref = refs
    else:
        dk_before_ref, dv_before_ref, dq_ref, dk_ref, dv_ref, d_bias_ref = refs
    samples, depth = q_ref.shape[1:3]
    sources, _, rows, crop = bias_ref.shape
    scaling = 1.0 / math.sqrt(depth)
    bias = bias_ref[:, 0].astype(F32).reshape(sources * rows, crop)
    valid = valid_ref[...] > 0
    total = jnp.zeros_like(bias)
    for s in range(samples):
        query, key, value = q_ref[0, s], k_ref[0, s], v_ref[0, s]
        grad_half = (weight_ref[s] * g_ref[0, s].astype(F32)).astype(BF16)
        scores = mm(query, key, 0, 0) * scaling + bias
        scores = jnp.where(valid, scores, masked_score)
        exp_scores = jnp.exp(scores - jnp.max(scores, -1, keepdims=True))
        attention = exp_scores / jnp.sum(exp_scores, -1, keepdims=True)
        d_attention = mm(grad_half, value, 0, 0)
        d_scores = attention * (
            d_attention - jnp.sum(attention * d_attention, -1, keepdims=True)
        )
        total = total + d_scores
        scores_half = d_scores.astype(BF16)
        d_value = mm(grad_half, attention.astype(BF16))
        d_key = mm(query, scores_half)
        dq_ref[0, s] = (mm(key, scores_half, 1, 1) * scaling).astype(BF16)
        if not first:
            d_value = d_value + dv_before_ref[0, s]
            d_key = d_key + dk_before_ref[0, s]
        if last:
            d_key = d_key * scaling
        dv_ref[0, s] = d_value.astype(dv_ref.dtype)
        dk_ref[0, s] = d_key.astype(dk_ref.dtype)
    d_bias_ref[:, 0] = total.astype(BF16).reshape(sources, rows, crop)


def attend_rows(first, last, weights, bias, valid, query, key, value, grad, state):
    sources, layers, rows, crop = bias.shape
    samples, depth, row_count = query.shape[1:]
    vec = lambda shape: pl.BlockSpec((1,) + shape[1:], lambda l: (l, 0, 0, 0))
    plane = pl.BlockSpec((sources, 1, rows, crop), lambda l: (0, l, 0, 0))
    in_specs = [
        pl.BlockSpec(memory_space=pltpu.SMEM),
        plane,
        pl.BlockSpec(valid.shape, lambda l: (0, 0)),
        vec(query.shape),
        vec(key.shape),
        vec(value.shape),
        vec(grad.shape),
    ]
    operands = [weights, bias, valid, query, key, value, grad]
    if not first:
        operands += list(state)
        in_specs += [vec(key.shape), vec(value.shape)]
    kind = BF16 if last else F32
    return pl.pallas_call(
        functools.partial(attend_kernel, first, last),
        grid=(layers,),
        in_specs=in_specs,
        out_specs=[vec(query.shape), vec(key.shape), vec(value.shape), plane],
        out_shape=[
            jax.ShapeDtypeStruct(query.shape, BF16),
            jax.ShapeDtypeStruct(key.shape, kind),
            jax.ShapeDtypeStruct(value.shape, kind),
            jax.ShapeDtypeStruct(bias.shape, BF16),
        ],
        compiler_params=pltpu.CompilerParams(vmem_limit_bytes=48 * 2**20),
        cost_estimate=pl.CostEstimate(
            flops=200 * layers * samples * depth * row_count * crop,
            bytes_accessed=layers * crop * (4 * row_count + 12 * samples * depth),
            transcendentals=layers * samples * row_count * crop,
        ),
        name="attention_backward",
    )(*operands)


def swap(array, teams=None):
    return lax.all_to_all(
        array, "tok", split_axis=0, concat_axis=0, tiled=True, axis_index_groups=teams
    )


def sum_pairs(keep, send):
    across = [(index, index ^ 1) for index in range(lax.axis_size("tok"))]
    return (keep + lax.ppermute(send, "tok", across).astype(F32)).astype(BF16)


def sum_team(array):
    devices = lax.axis_size("tok")
    teams = [list(range(odd, devices, 2)) for odd in range(2)]
    members = devices // 2
    parts = swap(array.reshape(members, array.shape[0] // members, array.shape[1]), teams)
    return jnp.sum(parts.astype(F32), 0).astype(BF16)


def finish_kernel(parity_ref, mine_ref, theirs_ref, in_ref, out_ref, bias_ref):
    mine, theirs = mine_ref[...].astype(F32), theirs_ref[...].astype(F32)
    even = parity_ref[0] == 0
    summed = jnp.concatenate([jnp.where(even, mine, theirs), jnp.where(even, theirs, mine)], 0)
    done = in_ref.shape[1]
    in_ref[...] = summed[:done].T
    out_ref[...] = summed[done : done + out_ref.shape[0]]
    done += out_ref.shape[0]
    bias_ref[...] = summed[done : done + bias_ref.shape[0]]


def gather_sums(share, parity, width, lanes):
    devices = lax.axis_size("tok")
    members = devices // 2
    channels = share.shape[1]
    across = [(index, index ^ 1) for index in range(devices)]
    teams = [list(range(odd, devices, 2)) for odd in range(2)]
    mine = swap(jnp.broadcast_to(share[None], (members,) + share.shape), teams)
    mine = mine.reshape(members * share.shape[0], channels)
    theirs = lax.ppermute(mine, "tok", across)
    return pl.pallas_call(
        finish_kernel,
        in_specs=[
            pl.BlockSpec(memory_space=pltpu.SMEM),
            pl.BlockSpec(memory_space=pltpu.VMEM),
            pl.BlockSpec(memory_space=pltpu.VMEM),
        ],
        out_shape=[
            jax.ShapeDtypeStruct((channels, 2 * width), F32),
            jax.ShapeDtypeStruct((width, channels), F32),
            jax.ShapeDtypeStruct((lanes, channels), F32),
        ],
        compiler_params=pltpu.CompilerParams(vmem_limit_bytes=32 * 2**20),
        name="weight_grads",
    )(parity, mine, theirs)


def body(
    pair_states,
    weight_in,
    weight_out,
    weight_bias,
    key_mask,
    noise_level,
    query_states,
    key_states,
    value_states,
    output_grad,
):
    row_count, crop, channels = pair_states.shape
    layers, _, heads = weight_bias.shape
    width = weight_out.shape[0]
    devices = lax.axis_size("tok")
    groups = devices // heads
    samples, depth = query_states.shape[2:4]
    lanes = heads * layers
    sizes = [row_count]
    if row_count % 16 == 0:
        sizes = [row_count // 2] * 2
    w_bias = jnp.transpose(weight_bias, (0, 2, 1))

    group = lax.axis_index("tok") // heads
    weights = sample_weight(lax.dynamic_slice_in_dim(noise_level, group * samples, samples))
    valid = key_mask[None, :]

    def by_chunk(array):
        cut = array[:, 0].reshape(layers, samples, depth, devices, len(sizes), sizes[0])
        cut = jnp.transpose(cut, (4, 0, 1, 2, 3, 5))
        return cut.reshape(len(sizes), layers, samples, depth, devices * sizes[0])

    queries, grads = by_chunk(query_states), by_chunk(output_grad)

    sum_rows = 3 * width + lanes
    padded_rows = 8 * devices * -(-sum_rows // (8 * devices))
    parity = (lax.axis_index("tok") % 2).astype(jnp.int32).reshape(1)
    piece = split_width(width)
    two = jnp.asarray(2.0, BF16)
    columns = []
    for at in range(0, width, piece):
        columns.append(weight_in[:, at : at + piece])
        columns.append(weight_in[:, width + at : width + at + piece] * two)
    scaled = (jnp.concatenate(columns, 1), weight_out * jnp.asarray(0.5, BF16))
    rows = sizes[0]
    direct = is_direct(rows, crop)

    def forward(start, count, prepared):
        return forward_rows(start, count, pair_states, weight_in, weight_out, w_bias, prepared)

    def send_bias(bias):
        if direct:
            bias = bias.reshape(heads, layers, rows, crop)
        else:
            bias = jnp.transpose(bias.reshape(rows, layers, heads, crop), (2, 1, 0, 3))
        if groups > 1:
            bias = jnp.tile(bias, (groups, 1, 1, 1))
        return swap(bias)

    def attend(start, bias, state):
        if not direct:
            bias = jnp.transpose(bias, (1, 0, 2, 3)).reshape(1, layers, devices * rows, crop)
        *grads_made, d_bias = attend_rows(
            start == 0,
            start + rows == row_count,
            weights,
            bias,
            valid,
            queries[start // rows],
            key_states[:, 0],
            value_states[:, 0],
            grads[start // rows],
            state,
        )
        if not direct:
            d_bias = jnp.transpose(d_bias.reshape(layers, devices, rows, crop), (1, 0, 2, 3))
        return grads_made, d_bias

    def send_back(d_bias):
        d_bias = swap(d_bias)
        if groups > 1:
            d_bias = d_bias.reshape(groups, heads, layers, rows, crop).astype(F32)
            d_bias = jnp.sum(d_bias, 0).astype(BF16)
        if direct:
            return d_bias.reshape(lanes, rows, crop)
        return jnp.transpose(d_bias, (2, 1, 0, 3)).reshape(rows, lanes, crop)

    def backward(start, count, d_bias, prepared, state):
        weights_used = (*prepared, *scaled)
        return backward_rows(
            start,
            count,
            direct,
            padded_rows,
            pair_states,
            d_bias,
            w_bias,
            weights_used,
            state,
            parity,
        )

    bias, *prepared = forward(0, rows, None)
    arrived = [send_bias(bias)]
    for start in range(rows, row_count, rows):
        arrived.append(send_bias(*forward(start, rows, prepared)))
    d_queries, returned = [], []
    state = None
    for start, bias in zip(range(0, row_count, rows), arrived):
        (d_query, *state), d_bias = attend(start, bias, state)
        d_queries.append(d_query)
        returned.append(send_back(d_bias))
    d_key, d_value = state
    state = None
    for start, d_bias in zip(range(0, row_count, rows), returned):
        state = backward(start, rows, d_bias, prepared, state)
    pair_grad, _, keep, send = state

    share = sum_team(sum_pairs(keep, send))
    grad_in, grad_out, grad_bias = gather_sums(share, parity, width, lanes)
    grad_bias = jnp.transpose(grad_bias.reshape(layers, heads, channels), (0, 2, 1))

    d_queries = [part.reshape(layers, samples, depth, devices, rows) for part in d_queries]
    d_query = jnp.concatenate(d_queries, -1).reshape(query_states.shape)
    return (
        pair_grad,
        d_query,
        d_key[:, None],
        d_value[:, None],
        grad_in,
        grad_out,
        grad_bias,
    )


def solution(mesh):
    in_specs = (
        P(("job", "tok"), None, None),
        P(),
        P(),
        P(),
        P("job"),
        P("job"),
        P(None, "tok", "job", None, None),
        P(None, "tok", "job", None, None),
        P(None, "tok", "job", None, None),
        P(None, "tok", "job", None, None),
    )
    out_specs = (
        P(("job", "tok"), None, None),
        P(None, "tok", "job", None, None),
        P(None, "tok", "job", None, None),
        P(None, "tok", "job", None, None),
        P("job", None),
        P("job", None),
        P("job", None, None),
    )
    return jax.shard_map(body, mesh=mesh, in_specs=in_specs, out_specs=out_specs, check_vma=False)
```

profile of v0, /device:TPU:0, one launch (start us, length us, event | category | flops | bytes accessed | tf_op | source)
XLA Modules:
  0.0 153.6 jit_solution(12379620594721125419)
XLA Ops:
  0.6 10.5 %pair_forward.2 = (bf16[32,16,512]{2,1,0:T(8,128)(2,1)}, bf16[1024,128]{1,0:T(8,128)(2,1)}, bf16[128,512]{1,0:T(8,128)(2,1)}) custom-call(bf16[32,512,128]{2,1,0:T(8,128)(2,1)} %pair_ref.7, bf16[2,16,128]{2,1,0:T(8,128)(2,1)} %bitcast.56, bf16[128,1024]{1,0:T(8,128)(2,1)} %refs_0_.1, bf16[512,128]{1,0:T(8,128)(2,1)} %refs_1_.1), custom_call_target="tpu_custom_call" | custom-call | flops 9865003008 | bytes 2621440 | tf_op jit(solution)/shard_map/pair_forward/pallas_call | solution.py:180
  11.2 7.4 %all-to-all-start.1 = ((bf16[16,2,16,512]{3,2,1,0:T(8,128)(2,1)}), bf16[16,2,16,512]{3,2,1,0:T(8,128)(2,1)S(1)}, u32[]{:S(2)}, u32[]{:S(2)}) async-start(bf16[16,2,16,512]{3,2,1,0:T(8,128)(2,1)} %bitcast.54), calls=%async_computation.1 | async-start | bytes 1048576 | tf_op jit(solution)/shard_map/all_to_all | solution.py:447
  18.6 0.3 copy.22
  18.9 10.2 %pair_forward.3 = bf16[32,16,512]{2,1,0:T(8,128)(2,1)} custom-call(bf16[32,512,128]{2,1,0:T(8,128)(2,1)} %pair_ref.7, bf16[2,16,128]{2,1,0:T(8,128)(2,1)} %bitcast.57, bf16[1024,128]{1,0:T(8,128)(2,1)} %get-tuple-element.26.refs_0_.w_in_t_ref, bf16[128,512]{1,0:T(8,128)(2,1)} %get-tuple-element.27.refs_1_.w_out_t_ref), custom_call_target="tpu_custom_call" | custom-call | flops 9865003008 | bytes 2621440 | tf_op jit(solution)/shard_map/pair_forward/pallas_call | solution.py:180
  29.1 3.9 %all-to-all-done.1.bias_ref = bf16[16,2,16,512]{3,2,1,0:T(8,128)(2,1)S(1)} async-done(((bf16[16,2,16,512]{3,2,1,0:T(8,128)(2,1)}), bf16[16,2,16,512]{3,2,1,0:T(8,128)(2,1)S(1)}, u32[]{:S(2)}, u32[]{:S(2)}) %all-to-all-start.1) | async-done | bytes 524320 | tf_op jit(solution)/shard_map/all_to_all | solution.py:447
  33.0 4.1 %all-to-all-start = ((bf16[16,2,16,512]{3,2,1,0:T(8,128)(2,1)}), bf16[16,2,16,512]{3,2,1,0:T(8,128)(2,1)S(1)}, u32[]{:S(2)}, u32[]{:S(2)}) async-start(bf16[16,2,16,512]{3,2,1,0:T(8,128)(2,1)} %bitcast.51), calls=%async_computation | async-start | bytes 1048576 | tf_op jit(solution)/shard_map/all_to_all | solution.py:447
  37.2 0.1 copy.24.q_ref
  37.3 0.1 copy.26.q_ref
  37.5 0.3 copy.23
  37.8 0.1 copy.25.g_ref
  37.9 0.1 copy.27.g_ref
  38.1 4.3 %attention_backward.2 = (bf16[2,2,48,256]{3,2,1,0:T(8,128)(2,1)S(1)}, f32[2,2,48,512]{3,2,1,0:T(8,128)S(1)}, f32[2,2,48,512]{3,2,1,0:T(8,128)S(1)}, bf16[16,2,16,512]{3,2,1,0:T(8,128)(2,1)}) custom-call(f32[2]{0:T(128)S(1)} %multiply_divide_fusion.weight_ref, bf16[16,2,16,512]{3,2,1,0:T(8,128)(2,1)S(1)} %all-to-all-done.1.bias_ref, s32[1,512]{1,0:T(1,128)S(1)} %bitcast.39, ...), custom_call_target="tpu_custom_call" | custom-call | flops 5033164800 | bytes 2228224 | tf_op jit(solution)/shard_map/attention_backward/pallas_call | solution.py:425
  42.4 9.2 %all-to-all-done.bias_ref = bf16[16,2,16,512]{3,2,1,0:T(8,128)(2,1)S(1)} async-done(((bf16[16,2,16,512]{3,2,1,0:T(8,128)(2,1)}), bf16[16,2,16,512]{3,2,1,0:T(8,128)(2,1)S(1)}, u32[]{:S(2)}, u32[]{:S(2)}) %all-to-all-start) | async-done | bytes 524320 | tf_op jit(solution)/shard_map/all_to_all | solution.py:447
  51.6 4.1 %all-to-all-start.3 = ((bf16[16,2,16,512]{3,2,1,0:T(8,128)(2,1)}), bf16[16,2,16,512]{3,2,1,0:T(8,128)(2,1)S(1)}, u32[]{:S(2)}, u32[]{:S(2)}) async-start(bf16[16,2,16,512]{3,2,1,0:T(8,128)(2,1)} %get-tuple-element.32), calls=%async_computation.3 | async-start | bytes 1048576 | tf_op jit(solution)/shard_map/all_to_all | solution.py:447
  55.8 0.7 pad_maximum_fusion.1.w_back_ref
  56.5 0.7 broadcast_multiply_fusion.w_half_ref
  57.1 4.2 %attention_backward.3 = (bf16[2,2,48,256]{3,2,1,0:T(8,128)(2,1)S(1)}, bf16[2,2,48,512]{3,2,1,0:T(8,128)(2,1)}, bf16[2,2,48,512]{3,2,1,0:T(8,128)(2,1)}, bf16[16,2,16,512]{3,2,1,0:T(8,128)(2,1)}) custom-call(f32[2]{0:T(128)S(1)} %multiply_divide_fusion.weight_ref, bf16[16,2,16,512]{3,2,1,0:T(8,128)(2,1)S(1)} %all-to-all-done.bias_ref, s32[1,512]{1,0:T(1,128)S(1)} %bitcast.40, ...), custom_call_target="tpu_custom_call" | custom-call | flops 5033164800 | bytes 2228224 | tf_op jit(solution)/shard_map/attention_backward/pallas_call | solution.py:425
  61.4 8.8 %all-to-all-done.3 = bf16[16,2,16,512]{3,2,1,0:T(8,128)(2,1)S(1)} async-done(((bf16[16,2,16,512]{3,2,1,0:T(8,128)(2,1)}), bf16[16,2,16,512]{3,2,1,0:T(8,128)(2,1)S(1)}, u32[]{:S(2)}, u32[]{:S(2)}) %all-to-all-start.3) | async-done | bytes 524320 | tf_op jit(solution)/shard_map/all_to_all | solution.py:447
  70.2 4.1 %all-to-all-start.2 = ((bf16[16,2,16,512]{3,2,1,0:T(8,128)(2,1)}), bf16[16,2,16,512]{3,2,1,0:T(8,128)(2,1)S(1)}, u32[]{:S(2)}, u32[]{:S(2)}) async-start(bf16[16,2,16,512]{3,2,1,0:T(8,128)(2,1)} %get-tuple-element.31), calls=%async_computation.2 | async-start | bytes 1048576 | tf_op jit(solution)/shard_map/all_to_all | solution.py:447
  74.3 23.7 %pair_backward.2 = (bf16[32,512,128]{2,1,0:T(8,128)(2,1)}, f32[1664,128]{1,0:T(8,128)}) custom-call(bf16[32,512,128]{2,1,0:T(8,128)(2,1)} %pair_ref.7, bf16[32,16,512]{2,1,0:T(8,128)(2,1)} %bitcast.52, bf16[2,16,128]{2,1,0:T(8,128)(2,1)} %bitcast.58, bf16[1024,128]{1,0:T(8,128)(2,1)} %get-tuple-element.26.refs_0_.w_in_t_ref, ...), custom_call_target="tpu_custom_call" | custom-call | flops 29393682432 | bytes 4718592 | tf_op jit(solution)/shard_map/pair_backward/pallas_call | solution.py:347
  98.0 0.8 copy-done.4
  98.8 24.3 %pair_backward.3 = (bf16[32,512,128]{2,1,0:T(8,128)(2,1)}, f32[1664,128]{1,0:T(8,128)}, f32[832,128]{1,0:T(8,128)}, bf16[832,128]{1,0:T(8,128)(2,1)}) custom-call(bf16[32,512,128]{2,1,0:T(8,128)(2,1)} %pair_ref.7, bf16[32,16,512]{2,1,0:T(8,128)(2,1)} %bitcast.53, bf16[2,16,128]{2,1,0:T(8,128)(2,1)} %bitcast.59, ...), custom_call_target="tpu_custom_call", output_to_operand_aliasing={{0}: (9, {})} | custom-call | flops 29393682432 | bytes 4718592 | tf_op jit(solution)/shard_map/pair_backward/pallas_call | solution.py:347
  123.2 0.5 collective-permute-start
  123.6 1.3 collective-permute-done
  124.9 1.1 add_convert_fusion
  126.0 14.2 %all_to_all.30 = bf16[8,104,128]{2,1,0:T(8,128)(2,1)S(1)} all-to-all(bf16[8,104,128]{2,1,0:T(8,128)(2,1)S(1)} %bitcast.50), channel_id=1, replica_groups={{0,2,4,6,8,10,12,14},{1,3,5,7,9,11,13,15},{16,18,20,22,24,26,28,30},{17..., dimensions={0} | all-to-all | bytes 425984 | tf_op jit(solution)/shard_map/all_to_all | solution.py:447
  140.2 11.0 %all_to_all.31 = bf16[8,104,128]{2,1,0:T(8,128)(2,1)S(1)} all-to-all(bf16[8,104,128]{2,1,0:T(8,128)(2,1)S(1)} %broadcast_in_dim.18), channel_id=1, replica_groups={{0,2,4,6,8,10,12,14},{1,3,5,7,9,11,13,15},{16,18,20,22,24,26,28,30},{17..., dimensions={0} | all-to-all | bytes 425984 | tf_op jit(solution)/shard_map/all_to_all | solution.py:447
  151.2 0.2 copy.29
  151.4 0.2 copy.28
  151.7 0.9 copy.31
  152.5 0.1 collective-permute-done.1.theirs_ref
  152.7 0.9 weight_grads.1
  (28 shorter events, 0.3 us)
Async XLA Ops:
  0.6 17.9 %copy-start.6 = (bf16[2,1,2,48,512]{4,3,2,1,0:T(8,128)(2,1)S(1)}, bf16[2,1,2,48,512]{4,3,2,1,0:T(8,128)(2,1)}, u32[]{:S(2)}) copy-start(bf16[2,1,2,48,512]{4,3,2,1,0:T(8,128)(2,1)} %param.16) | copy-start | bytes 589828
  11.2 21.9 %all-to-all-start.1 = ((bf16[16,2,16,512]{3,2,1,0:T(8,128)(2,1)}), bf16[16,2,16,512]{3,2,1,0:T(8,128)(2,1)S(1)}, u32[]{:S(2)}, u32[]{:S(2)}) async-start(bf16[16,2,16,512]{3,2,1,0:T(8,128)(2,1)} %bitcast.54), calls=%async_computation.1 | async-start | bytes 1048576 | tf_op jit(solution)/shard_map/all_to_all | solution.py:447
  18.9 18.6 %copy-start.7 = (bf16[2,1,2,48,512]{4,3,2,1,0:T(8,128)(2,1)S(1)}, bf16[2,1,2,48,512]{4,3,2,1,0:T(8,128)(2,1)}, u32[]{:S(2)}) copy-start(bf16[2,1,2,48,512]{4,3,2,1,0:T(8,128)(2,1)} %param.19) | copy-start | bytes 589828
  29.1 9.0 %copy-start.9 = (s32[2]{0:T(128)S(1)}, s32[2]{0:T(128)}, u32[]{:S(2)}) copy-start(s32[2]{0:T(128)} %param.15) | copy-start | bytes 28
  29.1 9.0 %copy-start = (bf16[2,1,2,48,512]{4,3,2,1,0:T(8,128)(2,1)S(1)}, bf16[2,1,2,48,512]{4,3,2,1,0:T(8,128)(2,1)}, u32[]{:S(2)}) copy-start(bf16[2,1,2,48,512]{4,3,2,1,0:T(8,128)(2,1)} %param.17) | copy-start | bytes 589828
  29.1 9.0 %copy-start.1 = (bf16[2,1,2,48,512]{4,3,2,1,0:T(8,128)(2,1)S(1)}, bf16[2,1,2,48,512]{4,3,2,1,0:T(8,128)(2,1)}, u32[]{:S(2)}) copy-start(bf16[2,1,2,48,512]{4,3,2,1,0:T(8,128)(2,1)} %param.18) | copy-start | bytes 589828
  29.1 9.0 %copy-start.2 = (s32[512]{0:T(512)S(1)}, s32[512]{0:T(512)}, u32[]{:S(2)}) copy-start(s32[512]{0:T(512)} %param.14) | copy-start | bytes 6148
  33.0 18.6 %all-to-all-start = ((bf16[16,2,16,512]{3,2,1,0:T(8,128)(2,1)}), bf16[16,2,16,512]{3,2,1,0:T(8,128)(2,1)S(1)}, u32[]{:S(2)}, u32[]{:S(2)}) async-start(bf16[16,2,16,512]{3,2,1,0:T(8,128)(2,1)} %bitcast.51), calls=%async_computation | async-start | bytes 1048576 | tf_op jit(solution)/shard_map/all_to_all | solution.py:447
  38.1 17.6 %copy-start.5 = (bf16[128,1024]{1,0:T(8,128)(2,1)S(1)}, bf16[128,1024]{1,0:T(8,128)(2,1)}, u32[]{:S(2)}) copy-start(bf16[128,1024]{1,0:T(8,128)(2,1)} %refs_0_.1) | copy-start | bytes 786436
  38.1 18.4 %copy-start.8 = (bf16[512,128]{1,0:T(8,128)(2,1)S(1)}, bf16[512,128]{1,0:T(8,128)(2,1)}, u32[]{:S(2)}) copy-start(bf16[512,128]{1,0:T(8,128)(2,1)} %refs_1_.1) | copy-start | bytes 393220
  51.6 18.6 %all-to-all-start.3 = ((bf16[16,2,16,512]{3,2,1,0:T(8,128)(2,1)}), bf16[16,2,16,512]{3,2,1,0:T(8,128)(2,1)S(1)}, u32[]{:S(2)}, u32[]{:S(2)}) async-start(bf16[16,2,16,512]{3,2,1,0:T(8,128)(2,1)} %get-tuple-element.32), calls=%async_computation.3 | async-start | bytes 1048576 | tf_op jit(solution)/shard_map/all_to_all | solution.py:447
  70.2 4.1 %copy-start.3 = (bf16[16,2,16,512]{3,2,1,0:T(8,128)(2,1)}, bf16[16,2,16,512]{3,2,1,0:T(8,128)(2,1)S(1)}, u32[]{:S(2)}) copy-start(bf16[16,2,16,512]{3,2,1,0:T(8,128)(2,1)S(1)} %all-to-all-done.3) | copy-start | bytes 1572868
  70.2 27.8 %all-to-all-start.2 = ((bf16[16,2,16,512]{3,2,1,0:T(8,128)(2,1)}), bf16[16,2,16,512]{3,2,1,0:T(8,128)(2,1)S(1)}, u32[]{:S(2)}, u32[]{:S(2)}) async-start(bf16[16,2,16,512]{3,2,1,0:T(8,128)(2,1)} %get-tuple-element.31), calls=%async_computation.2 | async-start | bytes 1048576 | tf_op jit(solution)/shard_map/all_to_all | solution.py:447
  98.0 0.8 copy-start.4
  123.2 1.8 %collective-permute-start = (bf16[832,128]{1,0:T(8,128)(2,1)}, bf16[832,128]{1,0:T(8,128)(2,1)S(1)}, u32[]{:S(2)}, u32[]{:S(2)}) collective-permute-start(bf16[832,128]{1,0:T(8,128)(2,1)} %get-tuple-element.41), channel_id=1, source_target_pairs={{0,1},{1,0},{2,3},{3,2},{4,5},{5,4},{6,7},{7,6},{8,9},{9,8},{10,11... | collective-permute-start | bytes 638984 | tf_op jit(solution)/shard_map/ppermute | solution.py:454
  151.2 1.5 collective-permute-start.1
where the time goes:
time: 154 us
  Pallas kernels  78.3 us (51%)
  blocking collectives  25.1 us (16%)
  waiting for transfers between devices  23.3 us (15%)
  starting transfers between devices  20.2 us (13%)
  local copies, waits for them, and re-layouts  3.22 us (2%)
  other arithmetic  2.63 us (2%)
    pallas_call x2, Pallas kernels, backward_rows(): pl.pallas_call(functools.partial(backward_kernel, first, last, direct), g...  48.1 us
    all_to_all x2, blocking collectives, swap(): lax.all_to_all(array, 'tok', split_axis=0, concat_axis=0, tiled=True, axi...  25.1 us
    all_to_all x4, waiting for transfers between devices, swap(): lax.all_to_all(array, 'tok', split_axis=0, concat_axis=0, tiled=True, axi...  21.9 us
    pallas_call x2, Pallas kernels, forward_rows(): pl.pallas_call(functools.partial(forward_kernel, direct, first), grid=(ro...  20.7 us
    all_to_all x4, starting transfers between devices, swap(): lax.all_to_all(array, 'tok', split_axis=0, concat_axis=0, tiled=True, axi...  19.7 us
    pallas_call x2, Pallas kernels, attend_rows(): pl.pallas_call(functools.partial(attend_kernel, first, last), grid=(layer...  8.53 us
  transfers between devices with their start and end apart: 6, of which 5 were waited for; matrix products, arithmetic and copies ran while one was open for 3% of the time, Pallas kernels for 28%

commit v1 on v0

--- a/solution.py
+++ b/solution.py
@@ -92,7 +92,7 @@
         w_in_ref, w_out_ref = refs.pop(0), refs.pop(0)
     else:
         w_in_t_ref, w_out_t_ref = refs.pop(0), refs.pop(0)
-    bias_ref = refs.pop(0)
+    bias_ref, normed_ref, inv_ref = refs.pop(0), refs.pop(0), refs.pop(0)
     if first:
         w_in_t_ref, w_out_t_ref = refs.pop(0), refs.pop(0)
     lines_ref = refs.pop(0)
@@ -113,7 +113,10 @@
 
     def stages(row):
         pair_float = pair_ref[row].T.astype(F32)
-        normed_in = normalize(pair_float)[0].astype(BF16)
+        normed_float, inv_in = normalize(pair_float)
+        normed_in = normed_float.astype(BF16)
+        normed_ref[row, :channels, :] = normed_in
+        inv_ref[row, 0:1, :] = inv_in
         yield True
         hiddens = []
         for at in range(0, width, piece):
@@ -125,7 +128,10 @@
             yield True
         lifted = pair_float + mm(w_out_t_ref[...], jnp.concatenate(hiddens, 0))
         yield True
-        normed_out = normalize(lifted)[0].astype(BF16)
+        normed_float, inv_out = normalize(lifted)
+        normed_out = normed_float.astype(BF16)
+        normed_ref[row, channels:, :] = normed_out
+        inv_ref[row, 1:2, :] = inv_out
         yield True
         bias = mm(w_bias_ref[...].reshape(layers * heads, channels), normed_out)
         if direct:
@@ -172,6 +178,9 @@
         if direct
         else pl.BlockSpec((step, lanes, crop), lambda i: (i, 0, 0))
     ]
+    for height, kind in ((2 * channels, BF16), (2, F32)):
+        shapes.append(jax.ShapeDtypeStruct((rows, height, crop), kind))
+        out_specs.append(pl.BlockSpec((step, height, crop), lambda i: (i, 0, 0)))
     operands = [pair, w_bias, *((w_in, w_out) if first else prepared)]
     if first:
         for shape in (w_in.shape[::-1], w_out.shape[::-1]):
@@ -201,11 +210,11 @@
     first,
     last,
     direct,
-    pair_ref,
+    normed_ref,
+    inv_ref,
     d_bias_ref,
     w_bias_ref,
     w_in_t_ref,
-    w_out_t_ref,
     w_back_ref,
     w_half_ref,
     *refs,
@@ -221,7 +230,7 @@
     layers, heads, channels = w_bias_ref.shape
     lanes = layers * heads
     piece = split_width(width)
-    step = pair_ref.shape[0]
+    step = normed_ref.shape[0]
     one, two = jnp.asarray(1.0, BF16), jnp.asarray(2.0, BF16)
     first_row = pl.program_id(0) * step
 
@@ -252,10 +261,8 @@
         sums_ref[at : at + left.shape[0], :] += mm(left, right, 1, 1)
 
     def stages(row):
-        pair_float = pair_ref[row].T.astype(F32)
-        normed_float, inv_in = normalize(pair_float)
-        normed_in = normed_float.astype(BF16)
-        yield True
+        normed_in, normed_out = normed_ref[row, :channels, :], normed_ref[row, channels:, :]
+        inv_in, inv_out = inv_ref[row, 0:1, :], inv_ref[row, 1:2, :]
         kept = []
         for at in range(0, width, piece):
             half_gate = mm(w_in_t_ref[at : at + piece, :], normed_in)
@@ -268,16 +275,10 @@
             slope = one_plus * (one + half_gate * (two - one_plus)) * up_in
             kept.append((silu, slope, hidden))
             yield True
-        hidden = jnp.concatenate([hidden for _, _, hidden in kept], 0)
-        lifted = pair_float + mm(w_out_t_ref[...], hidden)
-        yield True
-        out_float, inv_out = normalize(lifted)
-        normed_out = out_float.astype(BF16)
-        yield True
         d_bias = read_lines(row)
         d_normed = mm(w_bias_ref[...].reshape(lanes, channels), d_bias, 0, 0)
         add_sums(3 * width, d_bias, normed_out)
-        d_lifted = norm_back(out_float, inv_out, d_normed)
+        d_lifted = norm_back(normed_out.astype(F32), inv_out, d_normed)
         lifted_half = d_lifted.astype(BF16)
         yield True
         d_normed_in = None
@@ -291,7 +292,7 @@
             part = mm(w_back_ref[:, 2 * at : 2 * at + 2 * piece], d_both)
             d_normed_in = part if d_normed_in is None else d_normed_in + part
             yield True
-        pair_grad = d_lifted + norm_back(normed_float, inv_in, d_normed_in)
+        pair_grad = d_lifted + norm_back(normed_in.astype(F32), inv_in, d_normed_in)
         pair_grad_ref[row] = pair_grad.astype(BF16).T
 
     for_groups(step, 8, lambda at, count: interleave(lambda i: stages(at + i), count, 0))
@@ -313,19 +314,24 @@
             send_ref[...] = sums_ref[other, :].astype(BF16)
 
 
-def backward_rows(start, rows, direct, sum_rows, pair, d_bias, w_bias, prepared, state, parity):
-    crop, channels = pair.shape[1:]
+def backward_rows(
+    start, rows, direct, sum_rows, shape, stored, d_bias, w_bias, prepared, state, parity
+):
+    crop, channels = shape[1:]
     layers, heads, _ = w_bias.shape
     lanes = layers * heads
-    width = prepared[3].shape[0]
+    width = prepared[2].shape[0]
     step = row_step(rows)
     first_step = start // step
     positions = rows * crop
-    first, last = start == 0, start + rows == pair.shape[0]
+    first, last = start == 0, start + rows == shape[0]
     pair_spec = pl.BlockSpec((step, crop, channels), lambda i: (first_step + i, 0, 0))
     line_spec = whole_spec(d_bias) if direct else pl.BlockSpec((step, lanes, crop), lambda i: (i, 0, 0))
-    operands = [pair, d_bias, w_bias, *prepared]
-    in_specs = [pair_spec, line_spec] + [whole_spec(array) for array in operands[2:]]
+    operands = [*stored, d_bias, w_bias, *prepared]
+    in_specs = [
+        pl.BlockSpec((step,) + array.shape[1:], lambda i: (i, 0, 0)) for array in stored
+    ]
+    in_specs += [line_spec] + [whole_spec(array) for array in operands[len(stored) + 1 :]]
     aliases = {}
     if last:
         operands.append(parity)
@@ -336,7 +342,7 @@
         in_specs += [whole_spec(sums), pl.BlockSpec(memory_space=pl.ANY)]
         aliases = {len(operands) - 1: 0}
     shapes = [
-        jax.ShapeDtypeStruct(pair.shape, BF16),
+        jax.ShapeDtypeStruct(shape, BF16),
         jax.ShapeDtypeStruct((sum_rows, channels), F32),
     ]
     if last:
@@ -356,8 +362,8 @@
         ],
         compiler_params=pltpu.CompilerParams(vmem_limit_bytes=56 * 2**20),
         cost_estimate=pl.CostEstimate(
-            flops=6 * positions * channels * (9 * width + 2 * lanes),
-            bytes_accessed=positions * (2 * channels + lanes) * 2,
+            flops=6 * positions * channels * (8 * width + 2 * lanes),
+            bytes_accessed=positions * (3 * channels + lanes) * 2,
             transcendentals=positions * width,
         ),
         name="pair_backward",
@@ -587,14 +593,15 @@
             return d_bias.reshape(lanes, rows, crop)
         return jnp.transpose(d_bias, (2, 1, 0, 3)).reshape(rows, lanes, crop)
 
-    def backward(start, count, d_bias, prepared, state):
-        weights_used = (*prepared, *scaled)
+    def backward(start, count, stored, d_bias, prepared, state):
+        weights_used = (prepared[0], *scaled)
         return backward_rows(
             start,
             count,
             direct,
             padded_rows,
-            pair_states,
+            pair_states.shape,
+            stored,
             d_bias,
             w_bias,
             weights_used,
@@ -602,10 +609,13 @@
             parity,
         )
 
-    bias, *prepared = forward(0, rows, None)
-    arrived = [send_bias(bias)]
+    bias, *kept, w_in_t, w_out_t = forward(0, rows, None)
+    prepared = (w_in_t, w_out_t)
+    arrived, stored = [send_bias(bias)], [kept]
     for start in range(rows, row_count, rows):
-        arrived.append(send_bias(*forward(start, rows, prepared)))
+        bias, *kept = forward(start, rows, prepared)
+        arrived.append(send_bias(bias))
+        stored.append(kept)
     d_queries, returned = [], []
     state = None
     for start, bias in zip(range(0, row_count, rows), arrived):
@@ -614,8 +624,8 @@
         returned.append(send_back(d_bias))
     d_key, d_value = state
     state = None
-    for start, d_bias in zip(range(0, row_count, rows), returned):
-        state = backward(start, rows, d_bias, prepared, state)
+    for start, kept, d_bias in zip(range(0, row_count, rows), stored, returned):
+        state = backward(start, rows, kept, d_bias, prepared, state)
     pair_grad, _, keep, send = state
 
     share = sum_team(sum_pairs(keep, send))

time: 154 us -> 150 us (0.974)
  Pallas kernels: 78.3 us -> 75.4 us
    pallas_call x2, Pallas kernels: 48.1 us -> 43 us  [backward_rows(): pl.pallas_call(functools.partial(backward_kernel, first, last, direct), g...]
    pallas_call x2, Pallas kernels: 20.7 us -> 22.9 us  [forward_rows(): pl.pallas_call(functools.partial(forward_kernel, direct, first), grid=(ro...]
  transfers between devices with their start and end apart: 6 -> 6, of which waited for: 5 -> 5; matrix products, arithmetic and copies ran while one was open for 3% -> 3% of each run, Pallas kernels for 28% -> 27%
where the time goes in v1:
time: 150 us
  Pallas kernels  75.4 us (50%)
  blocking collectives  25.1 us (17%)
  waiting for transfers between devices  22.1 us (15%)
  starting transfers between devices  20.2 us (13%)
  local copies, waits for them, and re-layouts  3.24 us (2%)
  other arithmetic  2.65 us (2%)
    pallas_call x2, Pallas kernels, backward_rows(): pl.pallas_call(functools.partial(backward_kernel, first, last, direct), g...  43 us
    all_to_all x2, blocking collectives, swap(): lax.all_to_all(array, 'tok', split_axis=0, concat_axis=0, tiled=True, axi...  25.1 us
    pallas_call x2, Pallas kernels, forward_rows(): pl.pallas_call(functools.partial(forward_kernel, direct, first), grid=(ro...  22.9 us
    all_to_all x4, waiting for transfers between devices, swap(): lax.all_to_all(array, 'tok', split_axis=0, concat_axis=0, tiled=True, axi...  20.7 us
    all_to_all x4, starting transfers between devices, swap(): lax.all_to_all(array, 'tok', split_axis=0, concat_axis=0, tiled=True, axi...  19.7 us
    pallas_call x2, Pallas kernels, attend_rows(): pl.pallas_call(functools.partial(attend_kernel, first, last), grid=(layer...  8.55 us
  transfers between devices with their start and end apart: 6, of which 5 were waited for; matrix products, arithmetic and copies ran while one was open for 3% of the time, Pallas kernels for 27%

profile of v1, /device:TPU:0, one launch (start us, length us, event | category | flops | bytes accessed | tf_op | source)
XLA Modules:
  0.0 149.7 jit_solution(8648408540529665179)
XLA Ops:
  0.6 11.6 %pair_forward.2 = (bf16[32,16,512]{2,1,0:T(8,128)(2,1)}, bf16[16,256,512]{2,1,0:T(8,128)(2,1)}, f32[16,2,512]{2,1,0:T(2,128)}, bf16[1024,128]{1,0:T(8,128)(2,1)}, bf16[128,512]{1,0:T(8,128)(2,1)}) custom-call(bf16[32,512,128]{2,1,0:T(8,128)(2,1)} %pair_ref.3, bf16[2,16,128]{2,1,0:T(8,128)(2,1)} %bitcast.56, bf16[128,1024]{1,0:T(8,128)(2,1)} %refs_0_.1, ...), custom_call_target="tpu_custom_call" | custom-call | flops 9865003008 | bytes 2621440 | tf_op jit(solution)/shard_map/pair_forward/pallas_call | solution.py:189
  12.3 7.4 %all-to-all-start.1 = ((bf16[16,2,16,512]{3,2,1,0:T(8,128)(2,1)}), bf16[16,2,16,512]{3,2,1,0:T(8,128)(2,1)S(1)}, u32[]{:S(2)}, u32[]{:S(2)}) async-start(bf16[16,2,16,512]{3,2,1,0:T(8,128)(2,1)} %bitcast.54), calls=%async_computation.1 | async-start | bytes 1048576 | tf_op jit(solution)/shard_map/all_to_all | solution.py:453
  19.7 0.3 copy.22
  20.0 11.3 %pair_forward.3 = (bf16[32,16,512]{2,1,0:T(8,128)(2,1)}, bf16[16,256,512]{2,1,0:T(8,128)(2,1)}, f32[16,2,512]{2,1,0:T(2,128)}) custom-call(bf16[32,512,128]{2,1,0:T(8,128)(2,1)} %pair_ref.3, bf16[2,16,128]{2,1,0:T(8,128)(2,1)} %bitcast.57, bf16[1024,128]{1,0:T(8,128)(2,1)} %get-tuple-element.31.refs_0_.w_in_t_ref, bf16[128,512]{1,0:T(8,128)(2,1)} %get-tuple-element.32.refs_1_), custom_call_target="tpu_custom_call" | custom-call | flops 9865003008 | bytes 2621440 | tf_op jit(solution)/shard_map/pair_forward/pallas_call | solution.py:189
  31.3 2.8 %all-to-all-done.1.bias_ref = bf16[16,2,16,512]{3,2,1,0:T(8,128)(2,1)S(1)} async-done(((bf16[16,2,16,512]{3,2,1,0:T(8,128)(2,1)}), bf16[16,2,16,512]{3,2,1,0:T(8,128)(2,1)S(1)}, u32[]{:S(2)}, u32[]{:S(2)}) %all-to-all-start.1) | async-done | bytes 524320 | tf_op jit(solution)/shard_map/all_to_all | solution.py:453
  34.2 4.1 %all-to-all-start = ((bf16[16,2,16,512]{3,2,1,0:T(8,128)(2,1)}), bf16[16,2,16,512]{3,2,1,0:T(8,128)(2,1)S(1)}, u32[]{:S(2)}, u32[]{:S(2)}) async-start(bf16[16,2,16,512]{3,2,1,0:T(8,128)(2,1)} %bitcast.51), calls=%async_computation | async-start | bytes 1048576 | tf_op jit(solution)/shard_map/all_to_all | solution.py:453
  38.3 0.1 copy.24.q_ref
  38.5 0.3 copy.23
  38.8 0.1 copy.25.g_ref
  38.9 0.1 copy.26.q_ref
  39.1 0.1 copy.27.g_ref
  39.3 4.3 %attention_backward.2 = (bf16[2,2,48,256]{3,2,1,0:T(8,128)(2,1)S(1)}, f32[2,2,48,512]{3,2,1,0:T(8,128)S(1)}, f32[2,2,48,512]{3,2,1,0:T(8,128)S(1)}, bf16[16,2,16,512]{3,2,1,0:T(8,128)(2,1)}) custom-call(f32[2]{0:T(128)S(1)} %multiply_divide_fusion.weight_ref, bf16[16,2,16,512]{3,2,1,0:T(8,128)(2,1)S(1)} %all-to-all-done.1.bias_ref, s32[1,512]{1,0:T(1,128)S(1)} %bitcast.39, ...), custom_call_target="tpu_custom_call" | custom-call | flops 5033164800 | bytes 2228224 | tf_op jit(solution)/shard_map/attention_backward/pallas_call | solution.py:431
  43.6 9.2 %all-to-all-done.bias_ref = bf16[16,2,16,512]{3,2,1,0:T(8,128)(2,1)S(1)} async-done(((bf16[16,2,16,512]{3,2,1,0:T(8,128)(2,1)}), bf16[16,2,16,512]{3,2,1,0:T(8,128)(2,1)S(1)}, u32[]{:S(2)}, u32[]{:S(2)}) %all-to-all-start) | async-done | bytes 524320 | tf_op jit(solution)/shard_map/all_to_all | solution.py:453
  52.7 4.1 %all-to-all-start.3 = ((bf16[16,2,16,512]{3,2,1,0:T(8,128)(2,1)}), bf16[16,2,16,512]{3,2,1,0:T(8,128)(2,1)S(1)}, u32[]{:S(2)}, u32[]{:S(2)}) async-start(bf16[16,2,16,512]{3,2,1,0:T(8,128)(2,1)} %get-tuple-element.42), calls=%async_computation.3 | async-start | bytes 1048576 | tf_op jit(solution)/shard_map/all_to_all | solution.py:453
  56.9 0.7 pad_maximum_fusion.1.w_back_ref
  57.6 0.7 broadcast_multiply_fusion.w_half_ref
  58.3 4.3 %attention_backward.3 = (bf16[2,2,48,256]{3,2,1,0:T(8,128)(2,1)S(1)}, bf16[2,2,48,512]{3,2,1,0:T(8,128)(2,1)}, bf16[2,2,48,512]{3,2,1,0:T(8,128)(2,1)}, bf16[16,2,16,512]{3,2,1,0:T(8,128)(2,1)}) custom-call(f32[2]{0:T(128)S(1)} %multiply_divide_fusion.weight_ref, bf16[16,2,16,512]{3,2,1,0:T(8,128)(2,1)S(1)} %all-to-all-done.bias_ref, s32[1,512]{1,0:T(1,128)S(1)} %bitcast.40, ...), custom_call_target="tpu_custom_call" | custom-call | flops 5033164800 | bytes 2228224 | tf_op jit(solution)/shard_map/attention_backward/pallas_call | solution.py:431
  62.6 8.7 %all-to-all-done.3 = bf16[16,2,16,512]{3,2,1,0:T(8,128)(2,1)S(1)} async-done(((bf16[16,2,16,512]{3,2,1,0:T(8,128)(2,1)}), bf16[16,2,16,512]{3,2,1,0:T(8,128)(2,1)S(1)}, u32[]{:S(2)}, u32[]{:S(2)}) %all-to-all-start.3) | async-done | bytes 524320 | tf_op jit(solution)/shard_map/all_to_all | solution.py:453
  71.3 4.1 %all-to-all-start.2 = ((bf16[16,2,16,512]{3,2,1,0:T(8,128)(2,1)}), bf16[16,2,16,512]{3,2,1,0:T(8,128)(2,1)S(1)}, u32[]{:S(2)}, u32[]{:S(2)}) async-start(bf16[16,2,16,512]{3,2,1,0:T(8,128)(2,1)} %get-tuple-element.39), calls=%async_computation.2 | async-start | bytes 1048576 | tf_op jit(solution)/shard_map/all_to_all | solution.py:453
  75.4 21.2 %pair_backward.2 = (bf16[32,512,128]{2,1,0:T(8,128)(2,1)}, f32[1664,128]{1,0:T(8,128)}) custom-call(bf16[16,256,512]{2,1,0:T(8,128)(2,1)} %get-tuple-element.40.normed_ref, f32[16,2,512]{2,1,0:T(2,128)} %get-tuple-element.41.inv_ref, bf16[32,16,512]{2,1,0:T(8,128)(2,1)} %bitcast.52, bf16[2,16,128]{2,1,0:T(8,128)(2,1)} %bitcast.58, ...), custom_call_target="tpu_custom_call" | custom-call | flops 26172456960 | bytes 6815744 | tf_op jit(solution)/shard_map/pair_backward/pallas_call | solution.py:353
  96.6 0.8 copy-done.4
  97.4 21.8 %pair_backward.3 = (bf16[32,512,128]{2,1,0:T(8,128)(2,1)}, f32[1664,128]{1,0:T(8,128)}, f32[832,128]{1,0:T(8,128)}, bf16[832,128]{1,0:T(8,128)(2,1)}) custom-call(bf16[16,256,512]{2,1,0:T(8,128)(2,1)} %get-tuple-element.33.normed_ref, f32[16,2,512]{2,1,0:T(2,128)} %get-tuple-element.34.inv_ref, ...), custom_call_target="tpu_custom_call", output_to_operand_aliasing={{0}: (9, {})} | custom-call | flops 26172456960 | bytes 6815744 | tf_op jit(solution)/shard_map/pair_backward/pallas_call | solution.py:353
  119.2 0.5 collective-permute-start
  119.7 1.3 collective-permute-done
  121.0 1.1 add_convert_fusion
  122.0 14.2 %all_to_all.30 = bf16[8,104,128]{2,1,0:T(8,128)(2,1)S(1)} all-to-all(bf16[8,104,128]{2,1,0:T(8,128)(2,1)S(1)} %bitcast.50), channel_id=1, replica_groups={{0,2,4,6,8,10,12,14},{1,3,5,7,9,11,13,15},{16,18,20,22,24,26,28,30},{17..., dimensions={0} | all-to-all | bytes 425984 | tf_op jit(solution)/shard_map/all_to_all | solution.py:453
  136.3 11.0 %all_to_all.31 = bf16[8,104,128]{2,1,0:T(8,128)(2,1)S(1)} all-to-all(bf16[8,104,128]{2,1,0:T(8,128)(2,1)S(1)} %broadcast_in_dim.18), channel_id=1, replica_groups={{0,2,4,6,8,10,12,14},{1,3,5,7,9,11,13,15},{16,18,20,22,24,26,28,30},{17..., dimensions={0} | all-to-all | bytes 425984 | tf_op jit(solution)/shard_map/all_to_all | solution.py:453
  147.3 0.2 copy.29
  147.4 0.2 copy.28
  147.6 0.1 pad_maximum_fusion
  147.7 0.9 copy.31
  148.7 0.9 weight_grads.1
  (28 shorter events, 0.3 us)
Async XLA Ops:
  0.6 19.1 %copy-start.6 = (bf16[2,1,2,48,512]{4,3,2,1,0:T(8,128)(2,1)S(1)}, bf16[2,1,2,48,512]{4,3,2,1,0:T(8,128)(2,1)}, u32[]{:S(2)}) copy-start(bf16[2,1,2,48,512]{4,3,2,1,0:T(8,128)(2,1)} %param.16) | copy-start | bytes 589828
  12.3 21.9 %all-to-all-start.1 = ((bf16[16,2,16,512]{3,2,1,0:T(8,128)(2,1)}), bf16[16,2,16,512]{3,2,1,0:T(8,128)(2,1)S(1)}, u32[]{:S(2)}, u32[]{:S(2)}) async-start(bf16[16,2,16,512]{3,2,1,0:T(8,128)(2,1)} %bitcast.54), calls=%async_computation.1 | async-start | bytes 1048576 | tf_op jit(solution)/shard_map/all_to_all | solution.py:453
  20.0 18.5 %copy-start.7 = (bf16[2,1,2,48,512]{4,3,2,1,0:T(8,128)(2,1)S(1)}, bf16[2,1,2,48,512]{4,3,2,1,0:T(8,128)(2,1)}, u32[]{:S(2)}) copy-start(bf16[2,1,2,48,512]{4,3,2,1,0:T(8,128)(2,1)} %param.19) | copy-start | bytes 589828
  31.3 7.9 %copy-start.9 = (s32[2]{0:T(128)S(1)}, s32[2]{0:T(128)}, u32[]{:S(2)}) copy-start(s32[2]{0:T(128)} %param.15) | copy-start | bytes 28
  31.3 7.9 %copy-start = (bf16[2,1,2,48,512]{4,3,2,1,0:T(8,128)(2,1)S(1)}, bf16[2,1,2,48,512]{4,3,2,1,0:T(8,128)(2,1)}, u32[]{:S(2)}) copy-start(bf16[2,1,2,48,512]{4,3,2,1,0:T(8,128)(2,1)} %param.17) | copy-start | bytes 589828
  31.3 7.9 %copy-start.1 = (bf16[2,1,2,48,512]{4,3,2,1,0:T(8,128)(2,1)S(1)}, bf16[2,1,2,48,512]{4,3,2,1,0:T(8,128)(2,1)}, u32[]{:S(2)}) copy-start(bf16[2,1,2,48,512]{4,3,2,1,0:T(8,128)(2,1)} %param.18) | copy-start | bytes 589828
  31.3 7.9 %copy-start.2 = (s32[512]{0:T(512)S(1)}, s32[512]{0:T(512)}, u32[]{:S(2)}) copy-start(s32[512]{0:T(512)} %param.14) | copy-start | bytes 6148
  34.2 18.6 %all-to-all-start = ((bf16[16,2,16,512]{3,2,1,0:T(8,128)(2,1)}), bf16[16,2,16,512]{3,2,1,0:T(8,128)(2,1)S(1)}, u32[]{:S(2)}, u32[]{:S(2)}) async-start(bf16[16,2,16,512]{3,2,1,0:T(8,128)(2,1)} %bitcast.51), calls=%async_computation | async-start | bytes 1048576 | tf_op jit(solution)/shard_map/all_to_all | solution.py:453
  39.3 17.6 %copy-start.5 = (bf16[128,1024]{1,0:T(8,128)(2,1)S(1)}, bf16[128,1024]{1,0:T(8,128)(2,1)}, u32[]{:S(2)}) copy-start(bf16[128,1024]{1,0:T(8,128)(2,1)} %refs_0_.1) | copy-start | bytes 786436
  39.3 18.4 %copy-start.8 = (bf16[512,128]{1,0:T(8,128)(2,1)S(1)}, bf16[512,128]{1,0:T(8,128)(2,1)}, u32[]{:S(2)}) copy-start(bf16[512,128]{1,0:T(8,128)(2,1)} %refs_1_.1) | copy-start | bytes 393220
  52.7 18.6 %all-to-all-start.3 = ((bf16[16,2,16,512]{3,2,1,0:T(8,128)(2,1)}), bf16[16,2,16,512]{3,2,1,0:T(8,128)(2,1)S(1)}, u32[]{:S(2)}, u32[]{:S(2)}) async-start(bf16[16,2,16,512]{3,2,1,0:T(8,128)(2,1)} %get-tuple-element.42), calls=%async_computation.3 | async-start | bytes 1048576 | tf_op jit(solution)/shard_map/all_to_all | solution.py:453
  71.3 4.1 %copy-start.3 = (bf16[16,2,16,512]{3,2,1,0:T(8,128)(2,1)}, bf16[16,2,16,512]{3,2,1,0:T(8,128)(2,1)S(1)}, u32[]{:S(2)}) copy-start(bf16[16,2,16,512]{3,2,1,0:T(8,128)(2,1)S(1)} %all-to-all-done.3) | copy-start | bytes 1572868
  71.3 25.3 %all-to-all-start.2 = ((bf16[16,2,16,512]{3,2,1,0:T(8,128)(2,1)}), bf16[16,2,16,512]{3,2,1,0:T(8,128)(2,1)S(1)}, u32[]{:S(2)}, u32[]{:S(2)}) async-start(bf16[16,2,16,512]{3,2,1,0:T(8,128)(2,1)} %get-tuple-element.39), calls=%async_computation.2 | async-start | bytes 1048576 | tf_op jit(solution)/shard_map/all_to_all | solution.py:453
  96.6 0.8 copy-start.4
  119.2 1.8 %collective-permute-start = (bf16[832,128]{1,0:T(8,128)(2,1)}, bf16[832,128]{1,0:T(8,128)(2,1)S(1)}, u32[]{:S(2)}, u32[]{:S(2)}) collective-permute-start(bf16[832,128]{1,0:T(8,128)(2,1)} %get-tuple-element.51), channel_id=1, source_target_pairs={{0,1},{1,0},{2,3},{3,2},{4,5},{5,4},{6,7},{7,6},{8,9},{9,8},{10,11... | collective-permute-start | bytes 638984 | tf_op jit(solution)/shard_map/ppermute | solution.py:460
  147.3 1.5 collective-permute-start.1

commit v2 on v1

--- a/solution.py
+++ b/solution.py
@@ -51,7 +51,7 @@
 
 
 def split_width(width):
-    return 256 if width % 256 == 0 else width
+    return 512 if width % 512 == 0 else width
 
 
 def interleave(make_stages, count, lag):

time: 150 us -> 150 us (level)
  no operation moved by 1% of the time
where the time goes in v2:
time: 150 us
  Pallas kernels  75.5 us (50%)
  blocking collectives  25.1 us (17%)
  waiting for transfers between devices  22.1 us (15%)
  starting transfers between devices  20.2 us (13%)
  local copies, waits for them, and re-layouts  3.23 us (2%)
  other arithmetic  2.64 us (2%)
    pallas_call x2, Pallas kernels, backward_rows(): pl.pallas_call(functools.partial(backward_kernel, first, last, direct), g...  42.9 us
    all_to_all x2, blocking collectives, swap(): lax.all_to_all(array, 'tok', split_axis=0, concat_axis=0, tiled=True, axi...  25.1 us
    pallas_call x2, Pallas kernels, forward_rows(): pl.pallas_call(functools.partial(forward_kernel, direct, first), grid=(ro...  23.1 us
    all_to_all x4, waiting for transfers between devices, swap(): lax.all_to_all(array, 'tok', split_axis=0, concat_axis=0, tiled=True, axi...  20.7 us
    all_to_all x4, starting transfers between devices, swap(): lax.all_to_all(array, 'tok', split_axis=0, concat_axis=0, tiled=True, axi...  19.7 us
    pallas_call x2, Pallas kernels, attend_rows(): pl.pallas_call(functools.partial(attend_kernel, first, last), grid=(layer...  8.54 us
  transfers between devices with their start and end apart: 6, of which 5 were waited for; matrix products, arithmetic and copies ran while one was open for 3% of the time, Pallas kernels for 27%

profile of v2, /device:TPU:0, one launch (start us, length us, event | category | flops | bytes accessed | tf_op | source)
XLA Modules:
  0.0 149.7 jit_solution(3486022682065824063)
XLA Ops:
  0.6 11.8 %pair_forward.2 = (bf16[32,16,512]{2,1,0:T(8,128)(2,1)}, bf16[16,256,512]{2,1,0:T(8,128)(2,1)}, f32[16,2,512]{2,1,0:T(2,128)}, bf16[1024,128]{1,0:T(8,128)(2,1)}, bf16[128,512]{1,0:T(8,128)(2,1)}) custom-call(bf16[32,512,128]{2,1,0:T(8,128)(2,1)} %pair_ref.3, bf16[2,16,128]{2,1,0:T(8,128)(2,1)} %bitcast.56, bf16[128,1024]{1,0:T(8,128)(2,1)} %refs_0_.1, ...), custom_call_target="tpu_custom_call" | custom-call | flops 9865003008 | bytes 2621440 | tf_op jit(solution)/shard_map/pair_forward/pallas_call | solution.py:189
  12.4 7.4 %all-to-all-start.1 = ((bf16[16,2,16,512]{3,2,1,0:T(8,128)(2,1)}), bf16[16,2,16,512]{3,2,1,0:T(8,128)(2,1)S(1)}, u32[]{:S(2)}, u32[]{:S(2)}) async-start(bf16[16,2,16,512]{3,2,1,0:T(8,128)(2,1)} %bitcast.54), calls=%async_computation.1 | async-start | bytes 1048576 | tf_op jit(solution)/shard_map/all_to_all | solution.py:453
  19.8 0.3 copy.22
  20.1 11.4 %pair_forward.3 = (bf16[32,16,512]{2,1,0:T(8,128)(2,1)}, bf16[16,256,512]{2,1,0:T(8,128)(2,1)}, f32[16,2,512]{2,1,0:T(2,128)}) custom-call(bf16[32,512,128]{2,1,0:T(8,128)(2,1)} %pair_ref.3, bf16[2,16,128]{2,1,0:T(8,128)(2,1)} %bitcast.57, bf16[1024,128]{1,0:T(8,128)(2,1)} %get-tuple-element.31.refs_0_.w_in_t_ref, bf16[128,512]{1,0:T(8,128)(2,1)} %get-tuple-element.32.refs_1_), custom_call_target="tpu_custom_call" | custom-call | flops 9865003008 | bytes 2621440 | tf_op jit(solution)/shard_map/pair_forward/pallas_call | solution.py:189
  31.5 2.8 %all-to-all-done.1.bias_ref = bf16[16,2,16,512]{3,2,1,0:T(8,128)(2,1)S(1)} async-done(((bf16[16,2,16,512]{3,2,1,0:T(8,128)(2,1)}), bf16[16,2,16,512]{3,2,1,0:T(8,128)(2,1)S(1)}, u32[]{:S(2)}, u32[]{:S(2)}) %all-to-all-start.1) | async-done | bytes 524320 | tf_op jit(solution)/shard_map/all_to_all | solution.py:453
  34.3 4.1 %all-to-all-start = ((bf16[16,2,16,512]{3,2,1,0:T(8,128)(2,1)}), bf16[16,2,16,512]{3,2,1,0:T(8,128)(2,1)S(1)}, u32[]{:S(2)}, u32[]{:S(2)}) async-start(bf16[16,2,16,512]{3,2,1,0:T(8,128)(2,1)} %bitcast.51), calls=%async_computation | async-start | bytes 1048576 | tf_op jit(solution)/shard_map/all_to_all | solution.py:453
  38.4 0.1 copy.24.q_ref
  38.6 0.3 copy.23
  38.9 0.1 copy.25.g_ref
  39.0 0.1 copy.26.q_ref
  39.2 0.1 copy.27.g_ref
  39.4 4.3 %attention_backward.2 = (bf16[2,2,48,256]{3,2,1,0:T(8,128)(2,1)S(1)}, f32[2,2,48,512]{3,2,1,0:T(8,128)S(1)}, f32[2,2,48,512]{3,2,1,0:T(8,128)S(1)}, bf16[16,2,16,512]{3,2,1,0:T(8,128)(2,1)}) custom-call(f32[2]{0:T(128)S(1)} %multiply_divide_fusion.weight_ref, bf16[16,2,16,512]{3,2,1,0:T(8,128)(2,1)S(1)} %all-to-all-done.1.bias_ref, s32[1,512]{1,0:T(1,128)S(1)} %bitcast.39, ...), custom_call_target="tpu_custom_call" | custom-call | flops 5033164800 | bytes 2228224 | tf_op jit(solution)/shard_map/attention_backward/pallas_call | solution.py:431
  43.7 9.2 %all-to-all-done.bias_ref = bf16[16,2,16,512]{3,2,1,0:T(8,128)(2,1)S(1)} async-done(((bf16[16,2,16,512]{3,2,1,0:T(8,128)(2,1)}), bf16[16,2,16,512]{3,2,1,0:T(8,128)(2,1)S(1)}, u32[]{:S(2)}, u32[]{:S(2)}) %all-to-all-start) | async-done | bytes 524320 | tf_op jit(solution)/shard_map/all_to_all | solution.py:453
  52.8 4.1 %all-to-all-start.3 = ((bf16[16,2,16,512]{3,2,1,0:T(8,128)(2,1)}), bf16[16,2,16,512]{3,2,1,0:T(8,128)(2,1)S(1)}, u32[]{:S(2)}, u32[]{:S(2)}) async-start(bf16[16,2,16,512]{3,2,1,0:T(8,128)(2,1)} %get-tuple-element.42), calls=%async_computation.3 | async-start | bytes 1048576 | tf_op jit(solution)/shard_map/all_to_all | solution.py:453
  57.0 0.7 pad_maximum_fusion.1.w_back_ref
  57.7 0.7 broadcast_multiply_fusion.w_half_ref
  58.4 4.3 %attention_backward.3 = (bf16[2,2,48,256]{3,2,1,0:T(8,128)(2,1)S(1)}, bf16[2,2,48,512]{3,2,1,0:T(8,128)(2,1)}, bf16[2,2,48,512]{3,2,1,0:T(8,128)(2,1)}, bf16[16,2,16,512]{3,2,1,0:T(8,128)(2,1)}) custom-call(f32[2]{0:T(128)S(1)} %multiply_divide_fusion.weight_ref, bf16[16,2,16,512]{3,2,1,0:T(8,128)(2,1)S(1)} %all-to-all-done.bias_ref, s32[1,512]{1,0:T(1,128)S(1)} %bitcast.40, ...), custom_call_target="tpu_custom_call" | custom-call | flops 5033164800 | bytes 2228224 | tf_op jit(solution)/shard_map/attention_backward/pallas_call | solution.py:431
  62.7 8.7 %all-to-all-done.3 = bf16[16,2,16,512]{3,2,1,0:T(8,128)(2,1)S(1)} async-done(((bf16[16,2,16,512]{3,2,1,0:T(8,128)(2,1)}), bf16[16,2,16,512]{3,2,1,0:T(8,128)(2,1)S(1)}, u32[]{:S(2)}, u32[]{:S(2)}) %all-to-all-start.3) | async-done | bytes 524320 | tf_op jit(solution)/shard_map/all_to_all | solution.py:453
  71.4 4.1 %all-to-all-start.2 = ((bf16[16,2,16,512]{3,2,1,0:T(8,128)(2,1)}), bf16[16,2,16,512]{3,2,1,0:T(8,128)(2,1)S(1)}, u32[]{:S(2)}, u32[]{:S(2)}) async-start(bf16[16,2,16,512]{3,2,1,0:T(8,128)(2,1)} %get-tuple-element.39), calls=%async_computation.2 | async-start | bytes 1048576 | tf_op jit(solution)/shard_map/all_to_all | solution.py:453
  75.5 21.1 %pair_backward.2 = (bf16[32,512,128]{2,1,0:T(8,128)(2,1)}, f32[1664,128]{1,0:T(8,128)}) custom-call(bf16[16,256,512]{2,1,0:T(8,128)(2,1)} %get-tuple-element.40.normed_ref, f32[16,2,512]{2,1,0:T(2,128)} %get-tuple-element.41.inv_ref, bf16[32,16,512]{2,1,0:T(8,128)(2,1)} %bitcast.52, bf16[2,16,128]{2,1,0:T(8,128)(2,1)} %bitcast.58, ...), custom_call_target="tpu_custom_call" | custom-call | flops 26172456960 | bytes 6815744 | tf_op jit(solution)/shard_map/pair_backward/pallas_call | solution.py:353
  96.6 0.8 copy-done.4
  97.4 21.8 %pair_backward.3 = (bf16[32,512,128]{2,1,0:T(8,128)(2,1)}, f32[1664,128]{1,0:T(8,128)}, f32[832,128]{1,0:T(8,128)}, bf16[832,128]{1,0:T(8,128)(2,1)}) custom-call(bf16[16,256,512]{2,1,0:T(8,128)(2,1)} %get-tuple-element.33.normed_ref, f32[16,2,512]{2,1,0:T(2,128)} %get-tuple-element.34.inv_ref, ...), custom_call_target="tpu_custom_call", output_to_operand_aliasing={{0}: (9, {})} | custom-call | flops 26172456960 | bytes 6815744 | tf_op jit(solution)/shard_map/pair_backward/pallas_call | solution.py:353
  119.2 0.5 collective-permute-start
  119.7 1.3 collective-permute-done
  121.0 1.1 add_convert_fusion
  122.0 14.2 %all_to_all.30 = bf16[8,104,128]{2,1,0:T(8,128)(2,1)S(1)} all-to-all(bf16[8,104,128]{2,1,0:T(8,128)(2,1)S(1)} %bitcast.50), channel_id=1, replica_groups={{0,2,4,6,8,10,12,14},{1,3,5,7,9,11,13,15},{16,18,20,22,24,26,28,30},{17..., dimensions={0} | all-to-all | bytes 425984 | tf_op jit(solution)/shard_map/all_to_all | solution.py:453
  136.3 11.0 %all_to_all.31 = bf16[8,104,128]{2,1,0:T(8,128)(2,1)S(1)} all-to-all(bf16[8,104,128]{2,1,0:T(8,128)(2,1)S(1)} %broadcast_in_dim.18), channel_id=1, replica_groups={{0,2,4,6,8,10,12,14},{1,3,5,7,9,11,13,15},{16,18,20,22,24,26,28,30},{17..., dimensions={0} | all-to-all | bytes 425984 | tf_op jit(solution)/shard_map/all_to_all | solution.py:453
  147.2 0.2 copy.29
  147.4 0.2 copy.28
  147.7 0.9 copy.31
  148.6 0.1 collective-permute-done.1.theirs_ref
  148.7 0.9 weight_grads.1
  (28 shorter events, 0.3 us)
Async XLA Ops:
  0.6 19.2 %copy-start.6 = (bf16[2,1,2,48,512]{4,3,2,1,0:T(8,128)(2,1)S(1)}, bf16[2,1,2,48,512]{4,3,2,1,0:T(8,128)(2,1)}, u32[]{:S(2)}) copy-start(bf16[2,1,2,48,512]{4,3,2,1,0:T(8,128)(2,1)} %param.16) | copy-start | bytes 589828
  12.4 21.9 %all-to-all-start.1 = ((bf16[16,2,16,512]{3,2,1,0:T(8,128)(2,1)}), bf16[16,2,16,512]{3,2,1,0:T(8,128)(2,1)S(1)}, u32[]{:S(2)}, u32[]{:S(2)}) async-start(bf16[16,2,16,512]{3,2,1,0:T(8,128)(2,1)} %bitcast.54), calls=%async_computation.1 | async-start | bytes 1048576 | tf_op jit(solution)/shard_map/all_to_all | solution.py:453
  20.1 18.5 %copy-start.7 = (bf16[2,1,2,48,512]{4,3,2,1,0:T(8,128)(2,1)S(1)}, bf16[2,1,2,48,512]{4,3,2,1,0:T(8,128)(2,1)}, u32[]{:S(2)}) copy-start(bf16[2,1,2,48,512]{4,3,2,1,0:T(8,128)(2,1)} %param.19) | copy-start | bytes 589828
  31.5 7.8 %copy-start.9 = (s32[2]{0:T(128)S(1)}, s32[2]{0:T(128)}, u32[]{:S(2)}) copy-start(s32[2]{0:T(128)} %param.15) | copy-start | bytes 28
  31.5 7.9 %copy-start = (bf16[2,1,2,48,512]{4,3,2,1,0:T(8,128)(2,1)S(1)}, bf16[2,1,2,48,512]{4,3,2,1,0:T(8,128)(2,1)}, u32[]{:S(2)}) copy-start(bf16[2,1,2,48,512]{4,3,2,1,0:T(8,128)(2,1)} %param.17) | copy-start | bytes 589828
  31.5 7.9 %copy-start.1 = (bf16[2,1,2,48,512]{4,3,2,1,0:T(8,128)(2,1)S(1)}, bf16[2,1,2,48,512]{4,3,2,1,0:T(8,128)(2,1)}, u32[]{:S(2)}) copy-start(bf16[2,1,2,48,512]{4,3,2,1,0:T(8,128)(2,1)} %param.18) | copy-start | bytes 589828
  31.5 7.9 %copy-start.2 = (s32[512]{0:T(512)S(1)}, s32[512]{0:T(512)}, u32[]{:S(2)}) copy-start(s32[512]{0:T(512)} %param.14) | copy-start | bytes 6148
  34.3 18.6 %all-to-all-start = ((bf16[16,2,16,512]{3,2,1,0:T(8,128)(2,1)}), bf16[16,2,16,512]{3,2,1,0:T(8,128)(2,1)S(1)}, u32[]{:S(2)}, u32[]{:S(2)}) async-start(bf16[16,2,16,512]{3,2,1,0:T(8,128)(2,1)} %bitcast.51), calls=%async_computation | async-start | bytes 1048576 | tf_op jit(solution)/shard_map/all_to_all | solution.py:453
  39.4 17.6 %copy-start.5 = (bf16[128,1024]{1,0:T(8,128)(2,1)S(1)}, bf16[128,1024]{1,0:T(8,128)(2,1)}, u32[]{:S(2)}) copy-start(bf16[128,1024]{1,0:T(8,128)(2,1)} %refs_0_.1) | copy-start | bytes 786436
  39.4 18.4 %copy-start.8 = (bf16[512,128]{1,0:T(8,128)(2,1)S(1)}, bf16[512,128]{1,0:T(8,128)(2,1)}, u32[]{:S(2)}) copy-start(bf16[512,128]{1,0:T(8,128)(2,1)} %refs_1_.1) | copy-start | bytes 393220
  52.8 18.6 %all-to-all-start.3 = ((bf16[16,2,16,512]{3,2,1,0:T(8,128)(2,1)}), bf16[16,2,16,512]{3,2,1,0:T(8,128)(2,1)S(1)}, u32[]{:S(2)}, u32[]{:S(2)}) async-start(bf16[16,2,16,512]{3,2,1,0:T(8,128)(2,1)} %get-tuple-element.42), calls=%async_computation.3 | async-start | bytes 1048576 | tf_op jit(solution)/shard_map/all_to_all | solution.py:453
  71.4 4.1 %copy-start.3 = (bf16[16,2,16,512]{3,2,1,0:T(8,128)(2,1)}, bf16[16,2,16,512]{3,2,1,0:T(8,128)(2,1)S(1)}, u32[]{:S(2)}) copy-start(bf16[16,2,16,512]{3,2,1,0:T(8,128)(2,1)S(1)} %all-to-all-done.3) | copy-start | bytes 1572868
  71.4 25.2 %all-to-all-start.2 = ((bf16[16,2,16,512]{3,2,1,0:T(8,128)(2,1)}), bf16[16,2,16,512]{3,2,1,0:T(8,128)(2,1)S(1)}, u32[]{:S(2)}, u32[]{:S(2)}) async-start(bf16[16,2,16,512]{3,2,1,0:T(8,128)(2,1)} %get-tuple-element.39), calls=%async_computation.2 | async-start | bytes 1048576 | tf_op jit(solution)/shard_map/all_to_all | solution.py:453
  96.6 0.8 copy-start.4
  119.2 1.8 %collective-permute-start = (bf16[832,128]{1,0:T(8,128)(2,1)}, bf16[832,128]{1,0:T(8,128)(2,1)S(1)}, u32[]{:S(2)}, u32[]{:S(2)}) collective-permute-start(bf16[832,128]{1,0:T(8,128)(2,1)} %get-tuple-element.51), channel_id=1, source_target_pairs={{0,1},{1,0},{2,3},{3,2},{4,5},{5,4},{6,7},{7,6},{8,9},{9,8},{10,11... | collective-permute-start | bytes 638984 | tf_op jit(solution)/shard_map/ppermute | solution.py:460
  147.2 1.5 collective-permute-start.1
